TPU v7x, 256 devices: a whole 4x4x8 slice. The times are simulated.
256 devices in a mesh: row: 16 (over z_lo, y, core), col: 16 (over z_hi, x).
Axes of the slice: x: 4, y: 4, z: 8 (z_hi: 4, z_lo: 2; z = z_hi * 2 + z_lo), core: 2. Of those that a mesh axis runs over, the one named last changes fastest.
Arguments:
- source_desc: bfloat16 [32768, 64], P('row', 'col'), may hold values from -9 to 9
- target_desc: bfloat16 [32768, 64], P('col'), may hold values from -9 to 9
- source_mass: bfloat16 [32768], P('row'), may hold values from 0.099609375 to 10
- target_mass: bfloat16 [32768], P('col'), may hold values from 0.099609375 to 10
Outputs:
- cross_source: float32 [32768], P('row')
- cross_target: float32 [32768], P('col')
- self_source: float32 [32768], P('row')
- self_target: float32 [32768], P('col')
All inputs are finite; a program needn't handle non-finite values.
Results may differ from a plain program's by a relative error of at most 0.0003.
Values may be sent and summed in bfloat16 or wider, within the bound.
A program may use at most 64 MiB of HBM per device.

v0:
```python
import math
import jax
import jax.numpy as jnp
from jax import lax
from jax.sharding import PartitionSpec as P

ITERS = 2
EPSILON = 0.25
REACH = 1.0
DAMPING = 1.0 / (1.0 + EPSILON / REACH)


def half_norms(points):
    wide = points.astype(jnp.float32)
    return 0.5 * jnp.sum(wide * wide, axis=1)


def tile_stats(
    left_desc, right_desc, left_norm, right_norm, left_weight, right_weight, want_rows, want_cols
):
    count = left_desc.shape[0]
    block = math.gcd(512, count)
    blocks = count // block
    width = left_desc.shape[1]
    right_count = right_desc.shape[0]
    inputs = (
        left_desc.reshape(blocks, block, width),
        left_norm.reshape(blocks, block),
        left_weight.reshape(blocks, block),
    )

    def advance(carry, pieces):
        piece_desc, piece_norm, piece_weight = pieces
        product = lax.dot_general(
            piece_desc, right_desc, (((1,), (1,)), ((), ())), preferred_element_type=jnp.float32
        )
        scaled = (piece_norm[:, None] + right_norm[None, :] - product) / EPSILON
        emitted = ()
        if want_rows:
            row_score = right_weight[None, :] - scaled
            row_top = jnp.max(row_score, axis=1)
            row_total = jnp.sum(jnp.exp(row_score - row_top[:, None]), axis=1)
            emitted = (row_top, row_total)
        if want_cols:
            col_top, col_total = carry
            col_score = piece_weight[:, None] - scaled
            fresh_top = jnp.maximum(col_top, jnp.max(col_score, axis=0))
            col_total = col_total * jnp.exp(col_top - fresh_top) + jnp.sum(
                jnp.exp(col_score - fresh_top[None, :]), axis=0
            )
            carry = (fresh_top, col_total)
        return (carry, emitted)

    if want_cols:
        start = (
            jnp.full((right_count,), -jnp.inf, jnp.float32),
            jnp.zeros((right_count,), jnp.float32),
        )
    else:
        start = ()
    carry, emitted = lax.scan(advance, start, inputs)
    rows_out = (emitted[0].reshape(count), emitted[1].reshape(count)) if want_rows else None
    cols_out = carry if want_cols else None
    return (rows_out, cols_out)


def reduce_col(maxima, totals):
    merged_top = lax.pmax(maxima, "col")
    merged_total = lax.psum(totals * jnp.exp(maxima - merged_top), "col")
    return merged_top + jnp.log(merged_total)


def reduce_row(maxima, totals):
    merged_top = lax.pmax(maxima, "row")
    merged_total = lax.psum(totals * jnp.exp(maxima - merged_top), "row")
    return merged_top + jnp.log(merged_total)


def body(source_desc, target_desc, source_mass, target_mass):
    row_devices = lax.axis_size("row")
    col_devices = lax.axis_size("col")
    row_index = lax.axis_index("row")
    col_index = lax.axis_index("col")
    tile_count = source_mass.shape[0]
    source_part = tile_count // col_devices
    target_part = target_desc.shape[0] // row_devices
    mass_piece = lax.dynamic_slice_in_dim(source_mass, col_index * source_part, source_part, 0)
    source_rows = lax.all_gather(source_desc, "col", axis=1, tiled=True)
    desc_piece = lax.dynamic_slice_in_dim(source_rows, col_index * source_part, source_part, 0)
    source_cols, source_col_mass = (
        lax.all_gather(desc_piece, "row", axis=0, tiled=True),
        lax.all_gather(mass_piece, "row", axis=0, tiled=True),
    )
    target_piece = lax.dynamic_slice_in_dim(target_desc, row_index * target_part, target_part, 0)
    target_mass_piece = lax.dynamic_slice_in_dim(
        target_mass, row_index * target_part, target_part, 0
    )
    target_rows, target_row_mass = (
        lax.all_gather(target_piece, "col", axis=0, tiled=True),
        lax.all_gather(target_mass_piece, "col", axis=0, tiled=True),
    )
    source_log = jnp.log(source_mass.astype(jnp.float32))
    source_col_log = jnp.log(source_col_mass.astype(jnp.float32))
    target_log = jnp.log(target_mass.astype(jnp.float32))
    target_row_log = jnp.log(target_row_mass.astype(jnp.float32))
    source_row_norm = half_norms(source_rows)
    source_col_norm = half_norms(source_cols)
    target_col_norm = half_norms(target_desc)
    target_row_norm = half_norms(target_rows)
    cross_source = jnp.zeros((tile_count,), jnp.float32)
    cross_target = jnp.zeros((target_desc.shape[0],), jnp.float32)
    self_source = jnp.zeros((tile_count,), jnp.float32)
    self_target = jnp.zeros((target_desc.shape[0],), jnp.float32)
    source_view = jnp.zeros((source_cols.shape[0],), jnp.float32)
    target_view = jnp.zeros((target_rows.shape[0],), jnp.float32)
    for iteration in range(ITERS):
        mirror_work = iteration + 1 < ITERS
        cross_rows, cross_cols = tile_stats(
            source_rows,
            target_desc,
            source_row_norm,
            target_col_norm,
            source_log + cross_source / EPSILON,
            target_log + cross_target / EPSILON,
            True,
            True,
        )
        source_self_rows, source_self_cols = tile_stats(
            source_rows,
            source_cols,
            source_row_norm,
            source_col_norm,
            source_log + self_source / EPSILON,
            source_col_log + source_view / EPSILON,
            True,
            mirror_work,
        )
        target_self_rows, target_self_cols = tile_stats(
            target_rows,
            target_desc,
            target_row_norm,
            target_col_norm,
            target_row_log + target_view / EPSILON,
            target_log + self_target / EPSILON,
            mirror_work,
            True,
        )
        col_maxima = [cross_rows[0], source_self_rows[0]]
        col_totals = [cross_rows[1], source_self_rows[1]]
        row_maxima = [cross_cols[0], target_self_cols[0]]
        row_totals = [cross_cols[1], target_self_cols[1]]
        if mirror_work:
            col_maxima.append(target_self_rows[0])
            col_totals.append(target_self_rows[1])
            row_maxima.append(source_self_cols[0])
            row_totals.append(source_self_cols[1])
        col_logs = reduce_col(jnp.concatenate(col_maxima), jnp.concatenate(col_totals))
        row_logs = reduce_row(jnp.concatenate(row_maxima), jnp.concatenate(row_totals))
        target_count = target_desc.shape[0]
        cross_source = 0.5 * cross_source + 0.5 * DAMPING * (-EPSILON * col_logs[:tile_count])
        self_source = 0.5 * self_source + 0.5 * DAMPING * (
            -EPSILON * col_logs[tile_count : 2 * tile_count]
        )
        cross_target = 0.5 * cross_target + 0.5 * DAMPING * (-EPSILON * row_logs[:target_count])
        self_target = 0.5 * self_target + 0.5 * DAMPING * (
            -EPSILON * row_logs[target_count : 2 * target_count]
        )
        if mirror_work:
            target_view = 0.5 * target_view + 0.5 * DAMPING * (
                -EPSILON * col_logs[2 * tile_count :]
            )
            source_view = 0.5 * source_view + 0.5 * DAMPING * (
                -EPSILON * row_logs[2 * target_count :]
            )
    return (cross_source, cross_target, self_source, self_target)


def solution(mesh):
    return jax.shard_map(
        body,
        mesh=mesh,
        in_specs=(P("row", "col"), P("col", None), P("row"), P("col")),
        out_specs=(P("row"), P("col"), P("row"), P("col")),
        check_vma=False,
    )
```

profile of v0, /device:TPU:32, one launch (start us, length us, event | category | flops | bytes accessed | tf_op | source)
XLA Modules:
  0.0 824.4 jit_solution(18188859646712844108)
XLA Ops:
  0.6 47.2 %all-gather = bf16[16,4,2048]{2,1,0:T(4,128)(2,1)S(1)} all-gather(bf16[1,4,2048]{2,1,0:T(4,128)(2,1)} %bitcast.208), channel_id=1, replica_groups=mesh['row'=16,'col'=16] {'col'}, dimensions={0}, use_global_device_ids=true | all-gather | bytes 278528 | tf_op jit(solution)/shard_map/all_gather | solution.py:88
  47.9 20.2 %all_gather.16 = bf16[2048,64]{0,1:T(8,128)(2,1)S(1)} all-gather(bf16[128,64]{0,1:T(8,128)(2,1)S(1)} %dynamic-slice_bitcast_fusion), channel_id=1, replica_groups=mesh['row'=16,'col'=16] {'row'}, dimensions={0}, use_global_device_ids=true | all-gather | bytes 278528 | tf_op jit(solution)/shard_map/all_gather | solution.py:91
  69.3 16.1 %all-gather.1 = bf16[16,1,128]{2,1,0:T(2,128)(2,1)S(1)} all-gather(bf16[1,1,128]{2,1,0:T(2,128)(2,1)S(1)} %dynamic-slice_bitcast_fusion.2), channel_id=1, replica_groups=mesh['row'=16,'col'=16] {'row'}, dimensions={0}, use_global_device_ids=true | all-gather | bytes 4352 | tf_op jit(solution)/shard_map/all_gather | solution.py:92
  86.6 26.9 %while.95 = (s32[]{:T(128)}, f32[2048]{0:T(1024)S(1)}, f32[2048]{0:T(1024)S(1)}, f32[4,512]{1,0:T(4,128)S(1)}, f32[4,512]{1,0:T(4,128)S(1)}, /*index=5*/f32[4,51...) while((s32[]{:T(128)}, f32[2048]{0:T(1024)S(1)}, ...), condition=%wide.region_14.15_spmd.clone, body=%wide.region_9.14_spmd.clone.sunk | while | flops 147858432 | bytes 9203864 | solution.py:61
  89.8 3.4 exponential_reduce_fusion.18
  96.5 3.4 exponential_reduce_fusion.18
  103.3 3.4 exponential_reduce_fusion.18
  110.0 3.4 exponential_reduce_fusion.18
  113.7 26.7 %while.94 = (s32[]{:T(128)}, f32[2048]{0:T(1024)S(1)}, f32[2048]{0:T(1024)S(1)}, f32[4,512]{1,0:T(4,128)S(1)}, f32[4,512]{1,0:T(4,128)S(1)}, /*index=5*/f32[4,51...) while((s32[]{:T(128)}, f32[2048]{0:T(1024)S(1)}, ...), condition=%wide.region_7.8_spmd.clone, body=%wide.region_2.7_spmd.clone.sunk | while | flops 147858432 | bytes 8941720 | solution.py:61
  136.9 3.4 exponential_reduce_fusion.17
  140.5 39.3 %all_gather.19 = bf16[2048,64]{0,1:T(8,128)(2,1)S(1)} all-gather(bf16[128,64]{0,1:T(8,128)(2,1)S(1)} %constant_dynamic-slice_fusion.11), channel_id=1, replica_groups=mesh['row'=16,'col'=16] {'col'}, dimensions={0}, use_global_device_ids=true | all-gather | bytes 278528 | tf_op jit(solution)/shard_map/all_gather | solution.py:99
  180.3 39.8 %all-gather.2 = bf16[16,1,128]{2,1,0:T(2,128)(2,1)S(1)} all-gather(bf16[1,1,128]{2,1,0:T(2,128)(2,1)S(1)} %dynamic-slice_bitcast_fusion.1), channel_id=1, replica_groups=mesh['row'=16,'col'=16] {'col'}, dimensions={0}, use_global_device_ids=true | all-gather | bytes 4352 | tf_op jit(solution)/shard_map/all_gather | solution.py:100
  220.2 26.7 %while.96 = (s32[]{:T(128)}, f32[2048]{0:T(1024)S(1)}, f32[2048]{0:T(1024)S(1)}, f32[4,512]{1,0:T(4,128)S(1)}, f32[4,512]{1,0:T(4,128)S(1)}, /*index=5*/f32[4,51...) while((s32[]{:T(128)}, f32[2048]{0:T(1024)S(1)}, ...), condition=%wide.region_21.22_spmd.clone, body=%wide.region_16.21_spmd.clone.sunk | while | flops 147858432 | bytes 8941720 | solution.py:61
  246.9 76.7 %pmax.28 = f32[6144]{0:T(1024)S(1)} all-reduce(f32[6144]{0:T(1024)S(1)} %constant_dynamic-update-slice_fusion.8), channel_id=1, replica_groups=mesh['row'=16,'col'=16] {'col'}, use_global_device_ids=true, to_apply=%region_22.23 | all-reduce | flops 6144 | bytes 49152 | tf_op jit(solution)/shard_map/pmax | solution.py:68
  323.7 76.7 %psum.28 = f32[6144]{0:T(1024)S(1)} all-reduce(f32[6144]{0:T(1024)S(1)} %maximum_multiply_fusion), channel_id=1, replica_groups=mesh['row'=16,'col'=16] {'col'}, use_global_device_ids=true, to_apply=%region_23.24 | all-reduce | flops 6144 | bytes 49152 | tf_op jit(solution)/shard_map/psum | solution.py:69
  400.5 22.8 %while.98 = (s32[]{:T(128)}, f32[2048]{0:T(1024)S(1)}, f32[2048]{0:T(1024)S(1)}, f32[4,512]{1,0:T(4,128)S(1)}, f32[4,512]{1,0:T(4,128)S(1)}, /*index=5*/f32[2048...) while((s32[]{:T(128)}, f32[2048]{0:T(1024)S(1)}, ...), condition=%wide.region_41.42_spmd.clone, body=%wide.region_38.0_spmd.clone.sunk | while | flops 141568000 | bytes 8908920 | solution.py:61
  423.3 53.0 %pmax.29 = f32[6144]{0:T(1024)S(1)} all-reduce(f32[6144]{0:T(1024)S(1)} %constant_dynamic-update-slice_fusion.9), channel_id=1, replica_groups=mesh['row'=16,'col'=16] {'row'}, use_global_device_ids=true, to_apply=%region_24.25 | all-reduce | flops 6144 | bytes 49152 | tf_op jit(solution)/shard_map/pmax | solution.py:74
  476.3 53.1 %psum.29 = f32[6144]{0:T(1024)S(1)} all-reduce(f32[6144]{0:T(1024)S(1)} %maximum_multiply_fusion.1), channel_id=1, replica_groups=mesh['row'=16,'col'=16] {'row'}, use_global_device_ids=true, to_apply=%region_25.26 | all-reduce | flops 6144 | bytes 49152 | tf_op jit(solution)/shard_map/psum | solution.py:75
  529.5 26.7 %while.97 = (s32[]{:T(128)}, f32[2048]{0:T(1024)S(1)}, f32[2048]{0:T(1024)S(1)}, f32[4,512]{1,0:T(4,128)S(1)}, f32[4,512]{1,0:T(4,128)S(1)}, /*index=5*/f32[4,51...) while((s32[]{:T(128)}, f32[2048]{0:T(1024)S(1)}, ...), condition=%wide.region_31.32_spmd.clone, body=%wide.region_26.31_spmd.clone.sunk | while | flops 147858432 | bytes 8941720 | solution.py:61
  556.3 52.9 %pmax.31 = f32[4096]{0:T(1024)S(1)} all-reduce(f32[4096]{0:T(1024)S(1)} %constant_dynamic-update-slice_fusion.3), channel_id=1, replica_groups=mesh['row'=16,'col'=16] {'row'}, use_global_device_ids=true, to_apply=%region_42.43 | all-reduce | flops 4096 | bytes 32768 | tf_op jit(solution)/shard_map/pmax | solution.py:74
  609.2 52.9 %psum.31 = f32[4096]{0:T(1024)S(1)} all-reduce(f32[4096]{0:T(1024)S(1)} %maximum_multiply_fusion.3), channel_id=1, replica_groups=mesh['row'=16,'col'=16] {'row'}, use_global_device_ids=true, to_apply=%region_43.44 | all-reduce | flops 4096 | bytes 32768 | tf_op jit(solution)/shard_map/psum | solution.py:75
  662.8 7.4 while.93
  670.3 76.7 %pmax.30 = f32[4096]{0:T(1024)S(1)} all-reduce(f32[4096]{0:T(1024)S(1)} %constant_dynamic-update-slice_fusion.2), channel_id=1, replica_groups=mesh['row'=16,'col'=16] {'col'}, use_global_device_ids=true, to_apply=%region_36.37 | all-reduce | flops 4096 | bytes 32768 | tf_op jit(solution)/shard_map/pmax | solution.py:68
  747.0 76.7 %psum.30 = f32[4096]{0:T(1024)S(1)} all-reduce(f32[4096]{0:T(1024)S(1)} %maximum_multiply_fusion.2), channel_id=1, replica_groups=mesh['row'=16,'col'=16] {'col'}, use_global_device_ids=true, to_apply=%region_37.38 | all-reduce | flops 4096 | bytes 32768 | tf_op jit(solution)/shard_map/psum | solution.py:69
  (251 shorter events, 123.8 us)
Async XLA Ops:
  86.5 27.0 %copy-start = (bf16[2048,64]{0,1:T(8,128)(2,1)S(1)}, bf16[2048,64]{0,1:T(8,128)(2,1)}, u32[]{:S(2)}) copy-start(bf16[2048,64]{0,1:T(8,128)(2,1)} %param.17) | copy-start | bytes 786436
  86.6 27.1 %copy-start.1 = (bf16[2048]{0:T(1024)(128)(2,1)S(1)}, bf16[2048]{0:T(1024)(128)(2,1)}, u32[]{:S(2)}) copy-start(bf16[2048]{0:T(1024)(128)(2,1)} %param.19) | copy-start | bytes 12292
  220.2 180.3 %copy-start.2 = (bf16[2048]{0:T(1024)(128)(2,1)S(1)}, bf16[2048]{0:T(1024)(128)(2,1)}, u32[]{:S(2)}) copy-start(bf16[2048]{0:T(1024)(128)(2,1)} %param.18) | copy-start | bytes 12292
where the time goes:
time: 825 us; the launch traced here: 824 us
  blocking collectives  682 us (83%)
  other arithmetic  70.6 us (9%)
  matrix products  65.9 us (8%)
    pmax x2, blocking collectives, reduce_col(): merged_top = lax.pmax(maxima, 'col')  153 us
    psum x2, blocking collectives, reduce_col(): merged_total = lax.psum(totals * jnp.exp(maxima - merged_top), 'col')  153 us
    psum x2, blocking collectives, reduce_row(): merged_total = lax.psum(totals * jnp.exp(maxima - merged_top), 'row')  106 us
    pmax x2, blocking collectives, reduce_row(): merged_top = lax.pmax(maxima, 'row')  106 us
    dot_general x24, matrix products, advance(): lax.dot_general(piece_desc, right_desc, (((1,), (1,)), ((), ())), preferr...  65.9 us
    reduce_sum x20, other arithmetic, advance(): row_total = jnp.sum(jnp.exp(row_score - row_top[:, None]), axis=1)  56.8 us
    all_gather x1, blocking collectives, body(): source_rows = lax.all_gather(source_desc, 'col', axis=1, tiled=True)  47.2 us
    all_gather x1, blocking collectives, body(): lax.all_gather(target_mass_piece, 'col', axis=0, tiled=True)  39.8 us

commit v1 on v0

--- a/solution.py
+++ b/solution.py
@@ -72,7 +72,12 @@
 
 def reduce_row(maxima, totals):
     merged_top = lax.pmax(maxima, "row")
-    merged_total = lax.psum(totals * jnp.exp(maxima - merged_top), "row")
+
+    def link_the_strings(x0, dev_axis):
+        main = lax.all_gather(x0, dev_axis)
+        return jnp.sum(main, axis=0)
+
+    merged_total = link_the_strings(totals * jnp.exp(maxima - merged_top), "row")
     return merged_top + jnp.log(merged_total)
 
 

time: 825 us -> 756 us (0.916)
  blocking collectives: 682 us -> 611 us
    psum x2 -> x0, blocking collectives: 106 us -> none  [reduce_row(): merged_total = lax.psum(totals * jnp.exp(maxima - merged_top), 'row')]
    all_gather x0 -> x2, blocking collectives: none -> 33.9 us  [link_the_strings(): main = lax.all_gather(x0, dev_axis)]
where the time goes in v1:
time: 756 us; the launch traced here: 754 us
  blocking collectives  611 us (81%)
  other arithmetic  70.8 us (9%)
  matrix products  66.1 us (9%)
    pmax x2, blocking collectives, reduce_col(): merged_top = lax.pmax(maxima, 'col')  153 us
    psum x2, blocking collectives, reduce_col(): merged_total = lax.psum(totals * jnp.exp(maxima - merged_top), 'col')  153 us
    pmax x2, blocking collectives, reduce_row(): merged_top = lax.pmax(maxima, 'row')  108 us
    dot_general x24, matrix products, advance(): lax.dot_general(piece_desc, right_desc, (((1,), (1,)), ((), ())), preferr...  66.1 us
    reduce_sum x20, other arithmetic, advance(): row_total = jnp.sum(jnp.exp(row_score - row_top[:, None]), axis=1)  56.8 us
    all_gather x1, blocking collectives, body(): source_rows = lax.all_gather(source_desc, 'col', axis=1, tiled=True)  47.2 us
    all_gather x1, blocking collectives, body(): lax.all_gather(target_mass_piece, 'col', axis=0, tiled=True)  39.8 us
    all_gather x1, blocking collectives, body(): lax.all_gather(target_piece, 'col', axis=0, tiled=True)  39.3 us

profile of v1, /device:TPU:32, one launch (start us, length us, event | category | flops | bytes accessed | tf_op | source)
XLA Modules:
  0.0 754.5 jit_solution(1799257925833417564)
XLA Ops:
  0.6 47.2 %all-gather.2 = bf16[16,4,2048]{2,1,0:T(4,128)(2,1)S(1)} all-gather(bf16[1,4,2048]{2,1,0:T(4,128)(2,1)} %bitcast.208), channel_id=1, replica_groups=mesh['row'=16,'col'=16] {'col'}, dimensions={0}, use_global_device_ids=true | all-gather | bytes 278528 | tf_op jit(solution)/shard_map/all_gather | solution.py:93
  47.9 20.2 %all_gather.28 = bf16[2048,64]{0,1:T(8,128)(2,1)S(1)} all-gather(bf16[128,64]{0,1:T(8,128)(2,1)S(1)} %dynamic-slice_bitcast_fusion), channel_id=1, replica_groups=mesh['row'=16,'col'=16] {'row'}, dimensions={0}, use_global_device_ids=true | all-gather | bytes 278528 | tf_op jit(solution)/shard_map/all_gather | solution.py:96
  69.3 16.1 %all-gather.3 = bf16[16,1,128]{2,1,0:T(2,128)(2,1)S(1)} all-gather(bf16[1,1,128]{2,1,0:T(2,128)(2,1)S(1)} %dynamic-slice_bitcast_fusion.2), channel_id=1, replica_groups=mesh['row'=16,'col'=16] {'row'}, dimensions={0}, use_global_device_ids=true | all-gather | bytes 4352 | tf_op jit(solution)/shard_map/all_gather | solution.py:97
  86.6 27.0 %while.95 = (s32[]{:T(128)}, f32[2048]{0:T(1024)S(1)}, f32[2048]{0:T(1024)S(1)}, f32[4,512]{1,0:T(4,128)S(1)}, f32[4,512]{1,0:T(4,128)S(1)}, /*index=5*/f32[4,51...) while((s32[]{:T(128)}, f32[2048]{0:T(1024)S(1)}, ...), condition=%wide.region_14.15_spmd.clone, body=%wide.region_9.14_spmd.clone.sunk | while | flops 147858432 | bytes 9203864 | solution.py:61
  89.8 3.4 exponential_reduce_fusion.18
  113.7 26.8 %while.94 = (s32[]{:T(128)}, f32[2048]{0:T(1024)S(1)}, f32[2048]{0:T(1024)S(1)}, f32[4,512]{1,0:T(4,128)S(1)}, f32[4,512]{1,0:T(4,128)S(1)}, /*index=5*/f32[4,51...) while((s32[]{:T(128)}, f32[2048]{0:T(1024)S(1)}, ...), condition=%wide.region_7.8_spmd.clone, body=%wide.region_2.7_spmd.clone.sunk | while | flops 147858432 | bytes 8941720 | solution.py:61
  140.5 39.3 %all_gather.31 = bf16[2048,64]{0,1:T(8,128)(2,1)S(1)} all-gather(bf16[128,64]{0,1:T(8,128)(2,1)S(1)} %constant_dynamic-slice_fusion.11), channel_id=1, replica_groups=mesh['row'=16,'col'=16] {'col'}, dimensions={0}, use_global_device_ids=true | all-gather | bytes 278528 | tf_op jit(solution)/shard_map/all_gather | solution.py:104
  180.4 39.8 %all-gather.4 = bf16[16,1,128]{2,1,0:T(2,128)(2,1)S(1)} all-gather(bf16[1,1,128]{2,1,0:T(2,128)(2,1)S(1)} %dynamic-slice_bitcast_fusion.1), channel_id=1, replica_groups=mesh['row'=16,'col'=16] {'col'}, dimensions={0}, use_global_device_ids=true | all-gather | bytes 4352 | tf_op jit(solution)/shard_map/all_gather | solution.py:105
  220.2 26.8 %while.96 = (s32[]{:T(128)}, f32[2048]{0:T(1024)S(1)}, f32[2048]{0:T(1024)S(1)}, f32[4,512]{1,0:T(4,128)S(1)}, f32[4,512]{1,0:T(4,128)S(1)}, /*index=5*/f32[4,51...) while((s32[]{:T(128)}, f32[2048]{0:T(1024)S(1)}, ...), condition=%wide.region_21.22_spmd.clone, body=%wide.region_16.21_spmd.clone.sunk | while | flops 147858432 | bytes 8941720 | solution.py:61
  247.0 76.7 %pmax.28 = f32[6144]{0:T(1024)S(1)} all-reduce(f32[6144]{0:T(1024)S(1)} %constant_dynamic-update-slice_fusion.8), channel_id=1, replica_groups=mesh['row'=16,'col'=16] {'col'}, use_global_device_ids=true, to_apply=%region_22.23 | all-reduce | flops 6144 | bytes 49152 | tf_op jit(solution)/shard_map/pmax | solution.py:68
  323.8 76.7 %psum.14 = f32[6144]{0:T(1024)S(1)} all-reduce(f32[6144]{0:T(1024)S(1)} %maximum_multiply_fusion), channel_id=1, replica_groups=mesh['row'=16,'col'=16] {'col'}, use_global_device_ids=true, to_apply=%region_23.24 | all-reduce | flops 6144 | bytes 49152 | tf_op jit(solution)/shard_map/psum | solution.py:69
  400.6 22.8 %while.98 = (s32[]{:T(128)}, f32[2048]{0:T(1024)S(1)}, f32[2048]{0:T(1024)S(1)}, f32[4,512]{1,0:T(4,128)S(1)}, f32[4,512]{1,0:T(4,128)S(1)}, /*index=5*/f32[2048...) while((s32[]{:T(128)}, f32[2048]{0:T(1024)S(1)}, ...), condition=%wide.region_41.42_spmd.clone, body=%wide.region_38.0_spmd.clone.sunk | while | flops 141568000 | bytes 8908920 | solution.py:61
  423.4 53.0 %pmax.29 = f32[6144]{0:T(1024)S(1)} all-reduce(f32[6144]{0:T(1024)S(1)} %constant_dynamic-update-slice_fusion.9), channel_id=1, replica_groups=mesh['row'=16,'col'=16] {'row'}, use_global_device_ids=true, to_apply=%region_24.25 | all-reduce | flops 6144 | bytes 49152 | tf_op jit(solution)/shard_map/pmax | solution.py:74
  476.4 17.3 %all-gather = f32[98304]{0:T(1024)S(1)} all-gather(f32[6144]{0:T(1024)S(1)} %maximum_multiply_fusion.1), channel_id=2, replica_groups=mesh['row'=16,'col'=16] {'row'}, dimensions={0}, use_global_device_ids=true | all-gather | bytes 417792 | tf_op jit(solution)/shard_map/all_gather | solution.py:77
  493.9 26.8 %while.97 = (s32[]{:T(128)}, f32[2048]{0:T(1024)S(1)}, f32[2048]{0:T(1024)S(1)}, f32[4,512]{1,0:T(4,128)S(1)}, f32[4,512]{1,0:T(4,128)S(1)}, /*index=5*/f32[4,51...) while((s32[]{:T(128)}, f32[2048]{0:T(1024)S(1)}, ...), condition=%wide.region_31.32_spmd.clone, body=%wide.region_26.31_spmd.clone.sunk | while | flops 147858432 | bytes 8941720 | solution.py:61
  497.1 3.4 exponential_reduce_fusion.20
  503.8 3.4 exponential_reduce_fusion.20
  510.5 3.4 exponential_reduce_fusion.20
  517.2 3.4 exponential_reduce_fusion.20
  520.8 54.7 %pmax.31 = f32[4096]{0:T(1024)S(1)} all-reduce(f32[4096]{0:T(1024)S(1)} %constant_dynamic-update-slice_fusion.3), channel_id=1, replica_groups=mesh['row'=16,'col'=16] {'row'}, use_global_device_ids=true, to_apply=%region_42.43 | all-reduce | flops 4096 | bytes 32768 | tf_op jit(solution)/shard_map/pmax | solution.py:74
  575.5 16.7 %all-gather.1 = f32[65536]{0:T(1024)S(1)} all-gather(f32[4096]{0:T(1024)S(1)} %maximum_multiply_fusion.3), channel_id=3, replica_groups=mesh['row'=16,'col'=16] {'row'}, dimensions={0}, use_global_device_ids=true | all-gather | bytes 278528 | tf_op jit(solution)/shard_map/all_gather | solution.py:77
  592.9 7.5 while.93
  600.4 76.7 %pmax.30 = f32[4096]{0:T(1024)S(1)} all-reduce(f32[4096]{0:T(1024)S(1)} %constant_dynamic-update-slice_fusion.2), channel_id=1, replica_groups=mesh['row'=16,'col'=16] {'col'}, use_global_device_ids=true, to_apply=%region_36.37 | all-reduce | flops 4096 | bytes 32768 | tf_op jit(solution)/shard_map/pmax | solution.py:68
  677.1 76.7 %psum.15 = f32[4096]{0:T(1024)S(1)} all-reduce(f32[4096]{0:T(1024)S(1)} %maximum_multiply_fusion.2), channel_id=1, replica_groups=mesh['row'=16,'col'=16] {'col'}, use_global_device_ids=true, to_apply=%region_37.38 | all-reduce | flops 4096 | bytes 32768 | tf_op jit(solution)/shard_map/psum | solution.py:69
  (255 shorter events, 124.3 us)
Async XLA Ops:
  86.5 27.0 %copy-start = (bf16[2048,64]{0,1:T(8,128)(2,1)S(1)}, bf16[2048,64]{0,1:T(8,128)(2,1)}, u32[]{:S(2)}) copy-start(bf16[2048,64]{0,1:T(8,128)(2,1)} %param.17) | copy-start | bytes 786436
  86.6 27.1 %copy-start.1 = (bf16[2048]{0:T(1024)(128)(2,1)S(1)}, bf16[2048]{0:T(1024)(128)(2,1)}, u32[]{:S(2)}) copy-start(bf16[2048]{0:T(1024)(128)(2,1)} %param.19) | copy-start | bytes 12292
  220.2 180.3 %copy-start.2 = (bf16[2048]{0:T(1024)(128)(2,1)S(1)}, bf16[2048]{0:T(1024)(128)(2,1)}, u32[]{:S(2)}) copy-start(bf16[2048]{0:T(1024)(128)(2,1)} %param.18) | copy-start | bytes 12292
